TPU v7x, 128 devices: a whole 4x4x4 slice. The times are simulated.
128 devices in a mesh: tok: 4 (over x), voc: 8 (over z, core), section: 4 (over y).
Axes of the slice: x: 4, y: 4, z: 4, core: 2. Of those that a mesh axis runs over, the one named last changes fastest.
Arguments:
- hidden: bfloat16 [512, 4608], P('tok'), may hold values from -8 to 8
- head_weight: bfloat16 [128000, 4608], P(('tok', 'voc', 'section')), may hold values from -1 to 1
- teacher_logits: bfloat16 [512, 128000], P(('voc', 'section'), 'tok'), may hold values from -400 to 400
- token_weight: float32 [512], replicated, may hold values from 4 to 40
- token_ids: int32 [512], replicated, may hold values from 0 to 127999
- embed_grad: bfloat16 [512, 4608], P('tok'), may hold values from -6 to 6
Outputs:
- grad_hidden: bfloat16 [512, 4608], P('tok')
- grad_head: bfloat16 [128000, 4608], P(('tok', 'voc', 'section'))
All inputs are finite; a program needn't handle non-finite values.
Results may differ from a plain program's by a relative error of at most 0.0051.
Values may be sent and summed in bfloat16 or wider, within the bound.
A program may use at most 192 MiB of HBM per device.

v0:
```python
import functools

import jax
import jax.numpy as jnp
from jax import lax
from jax.experimental import pallas as pl
from jax.experimental.pallas import tpu as pltpu
from jax.sharding import PartitionSpec as P

MESH = pl.DeviceIdType.MESH
D = 4608
ROWS = 1000
WIDE = 1152
COLS = 32000
C = 768
HC = 384
H1, H2, H3 = 3, 9, 15
LOW = -1e30
F32 = jnp.float32
BF16 = jnp.bfloat16


def merge(tiles):
    top = functools.reduce(jnp.maximum, [t[0:4] for t in tiles])
    total = sum(t[4:8] * jnp.exp(t[0:4] - top) for t in tiles)
    return top, total


def kernel(hidden, weight, teacher, tw, ids, embed, gh_out, head_out,
           he, w, tl, tr, tT, sT, lhs, dl, st, tt, sr, trr,
           cs, cr, s1, r10, r11, r12, s20, s21, s22, r20, r21, r22,
           r30, r31, r32, go, ssem, rsem, lsem):
    x = lax.axis_index("tok")
    v = lax.axis_index("voc")
    y = lax.axis_index("section")
    z, c = v // 2, v % 2
    j = v * 4 + y
    zh, zl = z // 2, z % 2
    zcols = pl.ds(pl.multiple_of(zl * HC, 128), HC)
    zlanes = pl.ds(pl.multiple_of(zl * 128, 128), 128)

    def xp(d):
        return ((x + d) % 4, v, y)

    def yp(d):
        return (x, v, (y + d) % 4)

    def zp(d):
        return (x, (v + 2 * d) % 8, y)

    def xcp(a, b):
        return ((x + a) % 4, z * 2 + (c + b) % 2, y)

    def yzp(a, b):
        return (x, (v + 2 * b) % 8, (y + a) % 4)

    def pp(d):
        other = (j + d) % 32
        return (x, other // 4, other % 4)

    sibling = (x, v + 1 - 2 * c, y)
    count = [0]
    sent = []

    def send(src, dst, to):
        i = count[0]
        count[0] += 1
        copy = pltpu.make_async_remote_copy(
            src, dst, ssem.at[i], rsem.at[i], device_id=to, device_id_type=MESH)
        copy.start()
        sent.append(copy)
        return copy

    lcount = [0]

    def local(src, dst):
        i = lcount[0]
        lcount[0] += 1
        copy = pltpu.make_async_copy(src, dst, lsem.at[i])
        copy.start()
        return copy

    def arrive(copies):
        for copy in copies:
            copy.wait_recv()

    own_hidden = [local(hidden.at[:, :, :, pl.ds(k * C, C)], he.at[k, 0]) for k in range(6)]
    own_teacher = local(teacher, tl)
    own_weight = local(weight, w)
    own_embed = [local(embed.at[:, :, :, pl.ds(k * C, C)], he.at[k, 4]) for k in range(6)]

    barrier = pltpu.get_barrier_semaphore()
    for d in range(1, 4):
        pl.semaphore_signal(barrier, inc=1, device_id=xp(d), device_id_type=MESH)
        pl.semaphore_signal(barrier, inc=1, device_id=xcp(d, 1), device_id_type=MESH)
    for d in range(1, 32):
        pl.semaphore_signal(barrier, inc=1, device_id=pp(d), device_id_type=MESH)
    pl.semaphore_wait(barrier, 37)

    for copy in own_hidden:
        copy.wait()
    k0, k1, k2 = c * 3, c * 3 + 1, c * 3 + 2
    order = (1, 3, 2)
    hx = {}
    for k, p in ((k1, 1), (k2, 2)):
        hx[p] = [send(he.at[k, 0, y, zh, :, zcols], he.at[k, 4 - d, y, zh, :, zcols], xp(d)) for d in order]

    own_teacher.wait()
    def max_step(i, acc):
        for q in range(10):
            acc = jnp.maximum(acc, tl[:, pl.ds(pl.multiple_of((i * 10 + q) * 128, 128), 128)].astype(F32))
        return acc

    ttop = jnp.max(lax.fori_loop(0, COLS // 1280, max_step, jnp.full((16, 128), LOW, F32)), axis=1, keepdims=True)

    def sum_step(i, acc):
        for q in range(10):
            acc = acc + jnp.exp(tl[:, pl.ds(pl.multiple_of((i * 10 + q) * 128, 128), 128)].astype(F32) - ttop)
        return acc

    ttot = jnp.sum(lax.fori_loop(0, COLS // 1280, sum_step, jnp.zeros((16, 128), F32)), axis=1, keepdims=True)
    lane = lax.broadcasted_iota(jnp.int32, (16, 128), 1)
    row = lax.broadcasted_iota(jnp.int32, (16, 128), 0)
    here = lane == row + (j % 8) * 16
    tt[0, 0:4] = jnp.full((4, 128), LOW, F32)
    tt[0, 4:8] = jnp.zeros((4, 128), F32)
    tt[0, pl.ds(j // 8, 1)] = jnp.max(jnp.where(here, jnp.broadcast_to(ttop, (16, 128)), LOW), axis=0, keepdims=True)
    tt[0, pl.ds(4 + j // 8, 1)] = jnp.sum(jnp.where(here, jnp.broadcast_to(ttot, (16, 128)), 0.0), axis=0, keepdims=True)

    def stage(buf, rec, n, base, peers):
        return [send(buf.at[n], rec.at[base + i], peer) for i, peer in enumerate(peers)]

    def join(buf, rec, n, base, copies):
        arrive(copies)
        top, total = merge([buf[n]] + [rec[base + i] for i in range(len(copies))])
        buf[n + 1, 0:4] = top
        buf[n + 1, 4:8] = total

    xcpeers = [xcp(a, b) for a in (1, 3, 2, 0) for b in range(2) if a or b]
    yzpeers = [yzp(a, b) for a in (2, 1, 3, 0) for b in (2, 1, 3, 0) if a or b]
    ts = stage(tt, trr, 0, 0, xcpeers)
    hx[0] = [send(he.at[k0, 0], he.at[k0, 4 - d], xp(d)) for d in order]

    def start_of(device):
        return pl.multiple_of(jnp.minimum(device * ROWS // 128 * 128, COLS - WIDE), 128)

    teach = []

    def send_teacher(ds):
        for d in ds:
            teach.append(send(tl.at[:, pl.ds(start_of((j + d) % 32), WIDE)], tr.at[j], pp(d)))

    own_block = local(tl.at[:, pl.ds(start_of(j), WIDE)], tr.at[j])
    arrive(hx[1])
    part = he.at[k1, pl.ds(1, 3), y, zh, :, zcols]
    hy1 = [send(part, part, yp(d)) for d in order]
    arrive(hx[2])
    part = he.at[k2, pl.ds(1, 3), y, zh, :, zcols]
    hz2 = [send(part, part, zp(d)) for d in order]
    join(tt, trr, 0, 0, ts)
    ts = stage(tt, trr, 1, 7, yzpeers)
    arrive(hy1)
    part = he.at[k1, pl.ds(1, 3), :, zh, :, zcols]
    hz1 = [send(part, part, zp(d)) for d in order]
    arrive(hz2)
    part = he.at[k2, pl.ds(1, 3), y]
    hy2 = [send(part, part, yp(d)) for d in order]


    def student(k, first):
        for half in range(2):
            tok = he[k, 2 * half:2 * half + 2].reshape(256, C)
            cols = slice(half * 256, half * 256 + 256)
            part = lax.dot_general(w[:, pl.ds(pl.multiple_of(k * C, 128), C)], tok,
                                   (((1,), (1,)), ((), ())), preferred_element_type=F32)
            if first:
                sT[0:ROWS, cols] = part
            else:
                sT[0:ROWS, cols] += part

    arrive(hx[0])
    hc = [send(he.at[k0, pl.ds(1, 3)], he.at[k0, pl.ds(1, 3)], sibling)]
    for copy in own_embed:
        copy.wait()
    ex, ef = {}, {}


    def embed_near(p):
        k = c * 3 + p
        ex[p] = [send(he.at[k, 4], he.at[k, 8 - d], xp(d)) for d in (1, 3)]

    def embed_far(p):
        k = c * 3 + p
        arrive(ex[p])
        low, high = pl.ds(0, HC), pl.ds(HC, HC)
        ef[p] = [send(he.at[k, 5, :, :, :, low], he.at[k, 6, :, :, :, low], xp(3)),
                 send(he.at[k, 7, :, :, :, high], he.at[k, 6, :, :, :, high], xp(1))]

    embed_near(0)
    embed_near(1)
    own_weight.wait()
    student(k0, True)
    arrive(hz1)
    hc.append(send(he.at[k1, pl.ds(1, 3)], he.at[k1, pl.ds(1, 3)], sibling))
    arrive(hy2)
    hc.append(send(he.at[k2, pl.ds(1, 3)], he.at[k2, pl.ds(1, 3)], sibling))
    send_teacher(range(1, 32))
    arrive([hc[0]])
    student((1 - c) * 3, False)
    student(k1, False)
    student(k2, False)
    for p in range(1, 3):
        arrive([hc[p]])
        student((1 - c) * 3 + p, False)

    def smax_step(i, acc):
        block = sT[pl.ds(pl.multiple_of(i * 40, 8), 40), :]
        for q in range(5):
            acc = jnp.maximum(acc, block[q * 8:q * 8 + 8])
        return acc

    stop_ = jnp.max(lax.fori_loop(0, 25, smax_step, jnp.full((8, 512), -3e38, F32)), axis=0, keepdims=True)

    def ssum_step(i, acc):
        at = pl.ds(pl.multiple_of(i * 40, 8), 40)
        block = jnp.exp(sT[at, :] - stop_)
        sT[at, :] = block
        for q in range(5):
            acc = acc + block[q * 8:q * 8 + 8]
        return acc

    stot = jnp.sum(lax.fori_loop(0, 25, ssum_step, jnp.zeros((8, 512), F32)), axis=0, keepdims=True)
    blocks = [(x + r) % 4 for r in range(4)]
    for r in range(4):
        st[0, pl.ds(blocks[r], 1)] = stop_[:, r * 128:r * 128 + 128]
        st[0, pl.ds(4 + blocks[r], 1)] = stot[:, r * 128:r * 128 + 128]
    ss = stage(st, sr, 0, 0, xcpeers)

    lhs[ROWS - 8:1024, :] = jnp.zeros((1024 - ROWS + 8, 1024), BF16)
    idrow = jnp.concatenate([ids[pl.ds(blocks[r], 1), :] for r in range(4)], axis=1) - (x * COLS + j * ROWS)

    def onehot(i, _):
        at = pl.multiple_of(i * 32, 32)
        rows = lax.broadcasted_iota(jnp.int32, (32, 512), 0) + at
        lhs[pl.ds(at, 32), 512:1024] = jnp.where((rows == idrow) & (rows < ROWS), 1.0, 0.0).astype(BF16)
        return 0

    lax.fori_loop(0, 32, onehot, 0)
    join(st, sr, 0, 0, ss)
    ss = stage(st, sr, 1, 7, yzpeers)
    embed_far(0)
    embed_near(2)

    own_block.wait()
    arrive(teach)
    tT[:, WIDE:WIDE + 32, :] = jnp.zeros((4, 32, 128), F32)
    for r in range(4):
        at = pl.multiple_of(blocks[r] * 8, 8)
        for q in range(9):
            tile = tr[pl.ds(at, 8), :, q * 128:q * 128 + 128].reshape(128, 128).astype(F32)
            tT[r, q * 128:q * 128 + 128, :] = tile.T

    join(tt, trr, 1, 7, ts)
    join(st, sr, 1, 7, ss)

    weights = tw[...]
    st[3, 0:4] = weights / st[2, 4:8]
    tt[3, 0:4] = weights / tt[2, 4:8]

    def token_row(ref, n, base):
        return jnp.concatenate([ref[n, pl.ds(base + blocks[r], 1), :] for r in range(4)], axis=1)

    sfac = jnp.exp(stop_ - token_row(st, 2, 0)) * token_row(st, 3, 0)
    tfac = token_row(tt, 3, 0)
    tmax = token_row(tt, 2, 0)

    shift = j * ROWS - start_of(j)

    def dstep(i, _):
        at = pl.multiple_of(i * 128, 128)
        rows = lax.broadcasted_iota(jnp.int32, (128, 128), 0) + at
        for r in range(4):
            cols = slice(r * 128, r * 128 + 128)
            logit = tT[r, pl.ds(pl.multiple_of(shift + at, 8), 128), :]
            grad = sT[pl.ds(at, 128), cols] * sfac[:, cols] - jnp.exp(logit - tmax[:, cols]) * tfac[:, cols]
            grad = jnp.where(rows < ROWS, grad, 0.0)
            lhs[pl.ds(at, 128), cols] = grad.astype(BF16)
            dl[cols, pl.ds(at, 128)] = grad.T.astype(BF16)
        return 0

    lax.fori_loop(0, 8, dstep, 0)

    def ghpart(k, n):
        return jnp.dot(dl[:, 0:ROWS], w[:, pl.ds(pl.multiple_of(k * C + n * 256, 128), 256)],
                       preferred_element_type=F32)

    def zpart(d):
        oz = (z + d) % 4
        return oz // 2, pl.ds(pl.multiple_of((oz % 2) * 128, 128), 128)

    g1 = {0: [], 1: [], 2: []}
    gc = {}

    def theirs(n):
        for p in range(3):
            cs[p, n] = ghpart((1 - c) * 3 + p, n).astype(BF16)
        gc[n] = [send(cs.at[p, n], cr.at[p, n], sibling) for p in range(3)]

    def ours(n):
        arrive(gc[n])
        for p in range(3):
            mine = ghpart(c * 3 + p, n) + cr[p, n].astype(F32)
            s1[p, n] = mine.astype(BF16).reshape(4, 4, 2, 16, 256)
        for i, d in enumerate(order):
            g1[0].append(send(s1.at[0, n, d], r10.at[i, n], xp(d)))
            g1[1].append(send(s1.at[1, n, :, (y + d) % 4], r11.at[i, n], yp(d)))
            oh, ol = zpart(d)
            g1[2].append(send(s1.at[2, n, :, :, oh, :, ol], r12.at[i, n], zp(d)))

    theirs(0)
    theirs(1)
    ours(0)
    theirs(2)
    ours(1)
    ours(2)

    pieces = [(c * 3 + p, n) for p in range(3) for n in range(3)]
    pieces += [((1 - c) * 3 + p, n) for p in range(3) for n in range(3)]
    done = [0]

    def head(upto):
        for k, n in pieces[done[0]:upto]:
            both = he[k, :, :, :, :, n * 256:n * 256 + 256].reshape(1024, 256)
            head_out[:, pl.ds(pl.multiple_of(k * C + n * 256, 128), 256)] = jnp.dot(
                lhs[0:ROWS, :], both, preferred_element_type=F32).astype(BF16)
        done[0] = upto

    embed_far(1)
    embed_far(2)
    ec = []

    def embed_over(p):
        arrive(ef[p])
        ec.append(send(he.at[c * 3 + p, pl.ds(5, 3)], he.at[c * 3 + p, pl.ds(5, 3)], sibling))

    embed_over(0)
    head(H1)

    def total(own, rec):
        return (own.astype(F32) + sum(rec[i].astype(F32) for i in range(3))).astype(BF16)

    g2 = {}
    arrive(g1[0])
    s20[...] = total(s1[0, :, 0], r10)
    g2[0] = []
    for i, d in enumerate(order):
        oh, ol = zpart(d)
        g2[0].append(send(s20.at[:, :, oh, :, ol], r20.at[i], zp(d)))
    arrive(g1[1])
    s21[...] = total(s1[1, :, :, y], r11)
    g2[1] = [send(s21.at[:, d], r21.at[i], xp(d)) for i, d in enumerate(order)]
    arrive(g1[2])
    s22[...] = total(s1[2, :, :, :, zh, :, zlanes], r12)
    g2[2] = [send(s22.at[:, d], r22.at[i], xp(d)) for i, d in enumerate(order)]
    embed_over(1)
    embed_over(2)
    head(H2)
    arrive(ec)

    g3 = {}
    arrive(g2[0])
    r30[y] = total(s20[:, :, zh, :, zlanes], r20)
    g3[0] = [send(r30.at[y], r30.at[y], yp(d)) for d in order]
    arrive(g2[1])
    r31[z] = total(s21[:, 0], r21)
    g3[1] = [send(r31.at[z], r31.at[z], zp(d)) for d in order]
    arrive(g2[2])
    r32[y] = total(s22[:, 0], r22)
    g3[2] = [send(r32.at[y], r32.at[y], yp(d)) for d in order]
    head(H3)

    def all4(rec):
        return sum(rec[i].astype(F32) for i in range(4)).astype(BF16)

    g4 = {}
    arrive(g3[0])
    go[k0, :, :, zh, :, zlanes] = all4(r30)
    part = go.at[k0, :, :, zh, :, zlanes]
    g4[0] = [send(part, part, zp(d)) for d in order]
    arrive(g3[1])
    go[k1, :, y] = all4(r31)
    part = go.at[k1, :, y]
    g4[1] = [send(part, part, yp(d)) for d in order]
    arrive(g3[2])
    go[k2, :, :, zh, :, zlanes] = all4(r32)
    part = go.at[k2, :, :, zh, :, zlanes]
    g4[2] = [send(part, part, zp(d)) for d in order]
    head(18)
    last = []
    for p in range(3):
        arrive(g4[p])
        last.append(send(go.at[c * 3 + p], go.at[c * 3 + p], sibling))

    def finish(k):
        for n in range(3):
            gh_out[:, :, :, pl.ds(pl.multiple_of(k * C + n * 256, 128), 256)] = go[k, n]

    for p in range(3):
        finish(c * 3 + p)
    for p in range(3):
        arrive([last[p]])
        finish((1 - c) * 3 + p)
    for copy in sent:
        copy.wait_send()


def shards(hidden, head_weight, teacher_logits, token_weight, token_ids, embed_grad):
    anywhere = pl.BlockSpec(memory_space=pl.ANY)
    inside = pl.BlockSpec(memory_space=pltpu.VMEM)
    V = pltpu.VMEM
    gh, head = pl.pallas_call(
        kernel,
        out_shape=(V((4, 2, 16, D), BF16), V((ROWS, D), BF16)),
        in_specs=[anywhere, anywhere, anywhere, inside, inside, anywhere],
        out_specs=(inside, inside),
        scratch_shapes=[
            V((6, 8, 4, 2, 16, C), BF16),
            V((ROWS, D), BF16),
            V((16, COLS), BF16),
            V((32, 16, WIDE), BF16),
            V((4, WIDE + 32, 128), F32),
            V((1024, 512), F32),
            V((1024, 1024), BF16),
            V((512, 1024), BF16),
            V((4, 8, 128), F32),
            V((4, 8, 128), F32),
            V((22, 8, 128), F32),
            V((22, 8, 128), F32),
            V((3, 3, 512, 256), BF16),
            V((3, 3, 512, 256), BF16),
            V((3, 3, 4, 4, 2, 16, 256), BF16),
            V((3, 3, 4, 2, 16, 256), BF16),
            V((3, 3, 4, 2, 16, 256), BF16),
            V((3, 3, 4, 4, 16, 128), BF16),
            V((3, 4, 2, 16, 256), BF16),
            V((3, 4, 2, 16, 256), BF16),
            V((3, 4, 4, 16, 128), BF16),
            V((3, 3, 4, 16, 128), BF16),
            V((3, 3, 2, 16, 256), BF16),
            V((3, 3, 4, 16, 128), BF16),
            V((4, 3, 4, 16, 128), BF16),
            V((4, 3, 2, 16, 256), BF16),
            V((4, 3, 4, 16, 128), BF16),
            V((6, 3, 4, 2, 16, 256), BF16),
            pltpu.SemaphoreType.DMA((220,)),
            pltpu.SemaphoreType.DMA((220,)),
            pltpu.SemaphoreType.DMA((40,)),
        ],
        compiler_params=pltpu.CompilerParams(
            collective_id=0, has_side_effects=True, vmem_limit_bytes=48 * 2**20),
        cost_estimate=pl.CostEstimate(flops=19 * 10**9, bytes_accessed=30 * 10**6, transcendentals=2 * 10**6),
        name="distill",
    )(hidden.reshape(4, 2, 16, D), head_weight, teacher_logits, token_weight.reshape(4, 128),
      token_ids.astype(jnp.int32).reshape(4, 128), embed_grad.reshape(4, 2, 16, D))
    return gh.reshape(128, D), head


def solution(mesh):
    return jax.shard_map(
        shards,
        mesh=mesh,
        in_specs=(
            P("tok", None),
            P(("tok", "voc", "section"), None),
            P(("voc", "section"), "tok"),
            P(),
            P(),
            P("tok", None),
        ),
        out_specs=(P("tok", None), P(("tok", "voc", "section"), None)),
        check_vma=False,
    )
```

profile of v0, /device:TPU:1, one launch (start us, length us, event | category | flops | bytes accessed | tf_op | source)
XLA Modules:
  0.0 89.3 jit_solution(9310998295420717018)
XLA Ops:
  0.6 84.0 %distill.1 = (bf16[4,2,16,4608]{3,2,1,0:T(8,128)(2,1)S(1)}, bf16[1000,4608]{1,0:T(8,128)(2,1)S(1)}) custom-call(bf16[4,2,16,4608]{3,2,1,0:T(8,128)(2,1)} %bitcast.6, bf16[1000,4608]{1,0:T(8,128)(2,1)} %weight.1, bf16[16,32000]{1,0:T(8,128)(2,1)} %teacher.1, f32[4,128]{1,0:T(4,128)} %bitcast.8, s32[4,128]{1,0:T(4,128)} %bitcast.9, ...), custom_call_target="tpu_custom_call" | custom-call | flops 19000000512 | bytes 30000000 | tf_op jit(solution)/shard_map/distill/pallas_call | solution.py:421
  84.6 1.0 %copy.10 = bf16[128,4608]{1,0:T(8,128)(2,1)} copy(bf16[128,4608]{1,0:T(8,128)(2,1)S(1)} %bitcast.5) | data formatting | bytes 2359296
  85.6 3.7 %copy.11 = bf16[1000,4608]{1,0:T(8,128)(2,1)} copy(bf16[1000,4608]{1,0:T(8,128)(2,1)S(1)} %get-tuple-element.7) | data formatting | bytes 18432000
where the time goes:
time: 89.4 us; the launch traced here: 89.3 us
  Pallas kernels  84 us (94%)
  local copies, waits for them, and re-layouts  4.68 us (5%)
    pallas_call x1, Pallas kernels, shards(): pl.pallas_call(kernel, out_shape=(V((4, 2, 16, D), BF16), V((ROWS, D), BF...  84 us
    unnamed x2, local copies, waits for them, and re-layouts  4.68 us

commit v1 on v0

--- a/solution.py
+++ b/solution.py
@@ -14,6 +14,7 @@
 COLS = 32000
 C = 768
 HC = 384
+EARLY = 3
 H1, H2, H3 = 3, 9, 15
 LOW = -1e30
 F32 = jnp.float32
@@ -28,7 +29,7 @@
 
 def kernel(hidden, weight, teacher, tw, ids, embed, gh_out, head_out,
            he, w, tl, tr, tT, sT, lhs, dl, st, tt, sr, trr,
-           cs, cr, s1, r10, r11, r12, s20, s21, s22, r20, r21, r22,
+           cs, cr, mine, s1, r10, r11, r12, s20, s21, s22, r20, r21, r22,
            r30, r31, r32, go, ssem, rsem, lsem):
     x = lax.axis_index("tok")
     v = lax.axis_index("voc")
@@ -150,6 +151,7 @@
         for d in ds:
             teach.append(send(tl.at[:, pl.ds(start_of((j + d) % 32), WIDE)], tr.at[j], pp(d)))
 
+    send_teacher(range(1, 1 + EARLY))
     own_block = local(tl.at[:, pl.ds(start_of(j), WIDE)], tr.at[j])
     arrive(hx[1])
     part = he.at[k1, pl.ds(1, 3), y, zh, :, zcols]
@@ -162,9 +164,11 @@
     arrive(hy1)
     part = he.at[k1, pl.ds(1, 3), :, zh, :, zcols]
     hz1 = [send(part, part, zp(d)) for d in order]
+    over = {0: [], 1: [send(part, part, sibling)], 2: []}
     arrive(hz2)
     part = he.at[k2, pl.ds(1, 3), y]
     hy2 = [send(part, part, yp(d)) for d in order]
+    over[2].append(send(part, part, sibling))
 
 
     def student(k, first):
@@ -178,8 +182,9 @@
             else:
                 sT[0:ROWS, cols] += part
 
-    arrive(hx[0])
-    hc = [send(he.at[k0, pl.ds(1, 3)], he.at[k0, pl.ds(1, 3)], sibling)]
+    for copy, d in zip(hx[0], order):
+        arrive([copy])
+        over[0].append(send(he.at[k0, 4 - d], he.at[k0, 4 - d], sibling))
     for copy in own_embed:
         copy.wait()
     ex, ef = {}, {}
@@ -200,17 +205,21 @@
     embed_near(1)
     own_weight.wait()
     student(k0, True)
-    arrive(hz1)
-    hc.append(send(he.at[k1, pl.ds(1, 3)], he.at[k1, pl.ds(1, 3)], sibling))
-    arrive(hy2)
-    hc.append(send(he.at[k2, pl.ds(1, 3)], he.at[k2, pl.ds(1, 3)], sibling))
-    send_teacher(range(1, 32))
-    arrive([hc[0]])
+    for i, d in enumerate(order):
+        arrive([hz1[i]])
+        oz = (z - d + 4) % 4
+        part = he.at[k1, pl.ds(1, 3), :, oz // 2, :, pl.ds(pl.multiple_of((oz % 2) * HC, 128), HC)]
+        over[1].append(send(part, part, sibling))
+        arrive([hy2[i]])
+        part = he.at[k2, pl.ds(1, 3), (y - d + 4) % 4]
+        over[2].append(send(part, part, sibling))
+    send_teacher(range(1 + EARLY, 32))
+    arrive(over[0])
     student((1 - c) * 3, False)
     student(k1, False)
     student(k2, False)
     for p in range(1, 3):
-        arrive([hc[p]])
+        arrive(over[p])
         student((1 - c) * 3 + p, False)
 
     def smax_step(i, acc):
@@ -250,6 +259,7 @@
     ss = stage(st, sr, 1, 7, yzpeers)
     embed_far(0)
     embed_near(2)
+    embed_far(1)
 
     own_block.wait()
     arrive(teach)
@@ -299,30 +309,25 @@
         return oz // 2, pl.ds(pl.multiple_of((oz % 2) * 128, 128), 128)
 
     g1 = {0: [], 1: [], 2: []}
-    gc = {}
-
-    def theirs(n):
+    for n in range(3):
+        gc = []
         for p in range(3):
             cs[p, n] = ghpart((1 - c) * 3 + p, n).astype(BF16)
-        gc[n] = [send(cs.at[p, n], cr.at[p, n], sibling) for p in range(3)]
-
-    def ours(n):
-        arrive(gc[n])
+            gc.append(send(cs.at[p, n], cr.at[p, n], sibling))
         for p in range(3):
-            mine = ghpart(c * 3 + p, n) + cr[p, n].astype(F32)
-            s1[p, n] = mine.astype(BF16).reshape(4, 4, 2, 16, 256)
-        for i, d in enumerate(order):
-            g1[0].append(send(s1.at[0, n, d], r10.at[i, n], xp(d)))
-            g1[1].append(send(s1.at[1, n, :, (y + d) % 4], r11.at[i, n], yp(d)))
-            oh, ol = zpart(d)
-            g1[2].append(send(s1.at[2, n, :, :, oh, :, ol], r12.at[i, n], zp(d)))
-
-    theirs(0)
-    theirs(1)
-    ours(0)
-    theirs(2)
-    ours(1)
-    ours(2)
+            mine[p] = ghpart(c * 3 + p, n)
+        for p in range(3):
+            arrive([gc[p]])
+            both = mine[p] + cr[p, n].astype(F32)
+            s1[p, n] = both.astype(BF16).reshape(4, 4, 2, 16, 256)
+            for i, d in enumerate(order):
+                if p == 0:
+                    g1[0].append(send(s1.at[0, n, d], r10.at[i, n], xp(d)))
+                elif p == 1:
+                    g1[1].append(send(s1.at[1, n, :, (y + d) % 4], r11.at[i, n], yp(d)))
+                else:
+                    oh, ol = zpart(d)
+                    g1[2].append(send(s1.at[2, n, :, :, oh, :, ol], r12.at[i, n], zp(d)))
 
     pieces = [(c * 3 + p, n) for p in range(3) for n in range(3)]
     pieces += [((1 - c) * 3 + p, n) for p in range(3) for n in range(3)]
@@ -335,7 +340,6 @@
                 lhs[0:ROWS, :], both, preferred_element_type=F32).astype(BF16)
         done[0] = upto
 
-    embed_far(1)
     embed_far(2)
     ec = []
 
@@ -382,24 +386,31 @@
     def all4(rec):
         return sum(rec[i].astype(F32) for i in range(4)).astype(BF16)
 
-    g4 = {}
+    g4, last = {}, {}
     arrive(g3[0])
     go[k0, :, :, zh, :, zlanes] = all4(r30)
     part = go.at[k0, :, :, zh, :, zlanes]
     g4[0] = [send(part, part, zp(d)) for d in order]
+    last[0] = [send(part, part, sibling)]
     arrive(g3[1])
     go[k1, :, y] = all4(r31)
     part = go.at[k1, :, y]
     g4[1] = [send(part, part, yp(d)) for d in order]
+    last[1] = [send(part, part, sibling)]
     arrive(g3[2])
     go[k2, :, :, zh, :, zlanes] = all4(r32)
     part = go.at[k2, :, :, zh, :, zlanes]
     g4[2] = [send(part, part, zp(d)) for d in order]
+    last[2] = [send(part, part, sibling)]
     head(18)
-    last = []
-    for p in range(3):
-        arrive(g4[p])
-        last.append(send(go.at[c * 3 + p], go.at[c * 3 + p], sibling))
+    for i, d in enumerate(order):
+        oz = (z - d + 4) % 4
+        olanes = pl.ds(pl.multiple_of((oz % 2) * 128, 128), 128)
+        parts = [go.at[k0, :, :, oz // 2, :, olanes], go.at[k1, :, (y - d + 4) % 4],
+                 go.at[k2, :, :, oz // 2, :, olanes]]
+        for p in range(3):
+            arrive([g4[p][i]])
+            last[p].append(send(parts[p], parts[p], sibling))
 
     def finish(k):
         for n in range(3):
@@ -408,10 +419,21 @@
     for p in range(3):
         finish(c * 3 + p)
     for p in range(3):
-        arrive([last[p]])
+        arrive(last[p])
         finish((1 - c) * 3 + p)
     for copy in sent:
         copy.wait_send()
+
+
+def store(gh, head, gh_out, head_out, sems):
+    copies = [pltpu.make_async_copy(gh, gh_out, sems.at[9])]
+    for i in range(9):
+        at = pl.ds(i * 512, 512)
+        copies.append(pltpu.make_async_copy(head.at[:, at], head_out.at[:, at], sems.at[i]))
+    for copy in copies:
+        copy.start()
+    for copy in copies:
+        copy.wait()
 
 
 def shards(hidden, head_weight, teacher_logits, token_weight, token_ids, embed_grad):
@@ -438,6 +460,7 @@
             V((22, 8, 128), F32),
             V((3, 3, 512, 256), BF16),
             V((3, 3, 512, 256), BF16),
+            V((3, 512, 256), F32),
             V((3, 3, 4, 4, 2, 16, 256), BF16),
             V((3, 3, 4, 2, 16, 256), BF16),
             V((3, 3, 4, 2, 16, 256), BF16),
@@ -462,7 +485,16 @@
         name="distill",
     )(hidden.reshape(4, 2, 16, D), head_weight, teacher_logits, token_weight.reshape(4, 128),
       token_ids.astype(jnp.int32).reshape(4, 128), embed_grad.reshape(4, 2, 16, D))
-    return gh.reshape(128, D), head
+    return pl.pallas_call(
+        store,
+        out_shape=(jax.ShapeDtypeStruct((128, D), BF16), jax.ShapeDtypeStruct((ROWS, D), BF16)),
+        in_specs=[anywhere, anywhere],
+        out_specs=(anywhere, anywhere),
+        scratch_shapes=[pltpu.SemaphoreType.DMA((10,))],
+        compiler_params=pltpu.CompilerParams(vmem_limit_bytes=4 * 2**20),
+        cost_estimate=pl.CostEstimate(flops=0, bytes_accessed=10 * 2**20, transcendentals=0),
+        name="store",
+    )(gh.reshape(128, D), head)
 
 
 def solution(mesh):

time: 89.4 us -> 85.2 us (0.953)
  local copies, waits for them, and re-layouts: 4.68 us -> 0 us
    unnamed x2 -> x0, local copies, waits for them, and re-layouts: 4.68 us -> none
    pallas_call x0 -> x1, Pallas kernels: none -> 3.99 us  [shards(): pl.pallas_call(store, out_shape=(jax.ShapeDtypeStruct((128, D), BF16), ja...]
    pallas_call x1, Pallas kernels: 84 us -> 80.2 us  [shards(): pl.pallas_call(kernel, out_shape=(V((4, 2, 16, D), BF16), V((ROWS, D), BF...]
where the time goes in v1:
time: 85.2 us; the launch traced here: 85 us
  Pallas kernels  84.2 us (99%)
    pallas_call x1, Pallas kernels, shards(): pl.pallas_call(kernel, out_shape=(V((4, 2, 16, D), BF16), V((ROWS, D), BF...  80.2 us
    pallas_call x1, Pallas kernels, shards(): pl.pallas_call(store, out_shape=(jax.ShapeDtypeStruct((128, D), BF16), ja...  3.99 us

profile of v1, /device:TPU:1, one launch (start us, length us, event | category | flops | bytes accessed | tf_op | source)
XLA Modules:
  0.0 85.0 jit_solution(7530360475163259217)
XLA Ops:
  0.6 80.2 %distill.1 = (bf16[4,2,16,4608]{3,2,1,0:T(8,128)(2,1)S(1)}, bf16[1000,4608]{1,0:T(8,128)(2,1)S(1)}) custom-call(bf16[4,2,16,4608]{3,2,1,0:T(8,128)(2,1)} %bitcast.6, bf16[1000,4608]{1,0:T(8,128)(2,1)} %weight.1, bf16[16,32000]{1,0:T(8,128)(2,1)} %teacher.1, f32[4,128]{1,0:T(4,128)} %bitcast.8, s32[4,128]{1,0:T(4,128)} %bitcast.9, ...), custom_call_target="tpu_custom_call" | custom-call | flops 19000000512 | bytes 30000000 | tf_op jit(solution)/shard_map/distill/pallas_call | solution.py:443
  80.9 4.0 %store.1 = (bf16[128,4608]{1,0:T(8,128)(2,1)}, bf16[1000,4608]{1,0:T(8,128)(2,1)}) custom-call(bf16[128,4608]{1,0:T(8,128)(2,1)S(1)} %bitcast.5, bf16[1000,4608]{1,0:T(8,128)(2,1)S(1)} %get-tuple-element.5.head), custom_call_target="tpu_custom_call" | custom-call | bytes 10485760 | tf_op jit(solution)/shard_map/store/pallas_call | solution.py:488
